TPU v7x, 512 devices: a whole 4x4x16 slice. The times are simulated.
512 devices in a mesh: dp: 16 (over z), fsdp: 32 (over x, y, core).
Axes of the slice: x: 4, y: 4, z: 16, core: 2. Of those that a mesh axis runs over, the one named last changes fastest.
Arguments:
- prompt_hidden: bfloat16 [32768, 4096], P(('dp', 'fsdp')), may hold values from -6 to 6
- resp_hidden: bfloat16 [65536, 4096], P(('dp', 'fsdp')), may hold values from -6 to 6
- resp_query: bfloat16 [65536, 2048], P(('dp', 'fsdp')), may hold values from -80 to 80
- ln_gain: float32 [4096], replicated, may hold values from 0.25 to 1.75
- key_gain: float32 [128], replicated, may hold values from 0.1 to 1.9
- w_kv: bfloat16 [4096, 1024], P(('dp', 'fsdp')), may hold values from -0.09375 to 0.09375
- prompt_len: int32 [64], P('dp'), may hold values from 64 to 512, as said below
- resp_len: int32 [512], P(('dp', 'fsdp')), may hold values from 1 to 128, as said below
- owner: int32 [512], P(('dp', 'fsdp')), may hold values from 0 to 3, as said below
Outputs:
- attended: bfloat16 [65536, 2048], P(('dp', 'fsdp'))
Inputs may be any that keep to these rules, and one draw needn't show every extreme that they name: `prompt_len`: each group has one prompt of length exactly 512. `resp_len`: each group has one response of length exactly 128. `owner`: in each group every prompt index is named by exactly 8 responses.
All inputs are finite; a program needn't handle non-finite values.
Results may differ from a plain program's by a relative error of at most 0.014.
The roundings to bfloat16 on the way count: a program that leaves them out, or rounds other values in their place, can miss the bound.
Values may be sent and summed in bfloat16 or wider, within the bound.
A program may use at most 64 MiB of HBM per device.

v0:
```python
import jax
import jax.numpy as jnp
from jax import lax
from jax.sharding import PartitionSpec as P


def rms_scale(values, gain):
    mean_sq = jnp.mean(values * values, axis=-1, keepdims=True)
    return values * lax.rsqrt(mean_sq + 1e-06) * gain


def rotate(keys, positions, head_size):
    half = head_size // 2
    inv_freq = 1000000.0 ** (-(jnp.arange(half, dtype=jnp.float32) * 2.0) / head_size)
    angles = positions[:, None] * inv_freq[None, :]
    cosine = jnp.cos(angles)[:, None, :]
    sine = jnp.sin(angles)[:, None, :]
    first = keys[..., :half]
    second = keys[..., half:]
    return jnp.concatenate(
        [first * cosine - second * sine, second * cosine + first * sine], axis=-1
    )


def body(
    prompt_hidden, resp_hidden, resp_query, ln_gain, key_gain, w_kv, prompt_len, resp_len, owner
):
    head_size = key_gain.shape[0]
    kv_width = w_kv.shape[1] // 2
    kv_heads = kv_width // head_size
    query_heads = resp_query.shape[1] // head_size
    prompt_rows = prompt_hidden.shape[0]
    resp_rows = resp_hidden.shape[0]
    prompt_slots = prompt_len.shape[0]
    members = lax.axis_size("fsdp")
    sub_rows = prompt_rows // prompt_slots
    slot_len = sub_rows * members
    stacked = jnp.concatenate([prompt_hidden, resp_hidden], axis=0)
    normed = rms_scale(stacked.astype(jnp.float32), ln_gain).astype(jnp.bfloat16)
    kv = jnp.dot(
        normed,
        lax.all_gather(w_kv, ("dp", "fsdp"), axis=0, tiled=True),
        preferred_element_type=jnp.float32,
    )
    member = lax.axis_index("fsdp")
    prompt_index = owner[0]
    plen = prompt_len[prompt_index]
    local = jnp.arange(prompt_rows, dtype=jnp.int32)
    prompt_pos = (member * sub_rows + local % sub_rows).astype(jnp.float32)
    resp_pos = plen.astype(jnp.float32) + jnp.arange(resp_rows, dtype=jnp.float32)
    positions = jnp.concatenate([prompt_pos, resp_pos], axis=0)
    keys = kv[:, :kv_width].reshape(-1, kv_heads, head_size)
    keys = rotate(rms_scale(keys, key_gain), positions, head_size)
    cache = jnp.concatenate([keys.reshape(-1, kv_width), kv[:, kv_width:]], axis=-1).astype(
        jnp.bfloat16
    )
    prompt_cache = cache[:prompt_rows]
    own = cache[prompt_rows:]
    gathered = lax.all_gather(prompt_cache, "fsdp", axis=0, tiled=True)
    blocks = gathered.reshape(members, prompt_slots, sub_rows, 2 * kv_width)
    prefix = lax.dynamic_index_in_dim(blocks, prompt_index, 1, False).reshape(
        slot_len, 2 * kv_width
    )
    total_keys = slot_len + resp_rows
    all_keys = jnp.concatenate([prefix[:, :kv_width], own[:, :kv_width]], axis=0).reshape(
        total_keys, kv_heads, head_size
    )
    all_vals = jnp.concatenate([prefix[:, kv_width:], own[:, kv_width:]], axis=0).reshape(
        total_keys, kv_heads, head_size
    )
    queries = resp_query.reshape(resp_rows, kv_heads, query_heads // kv_heads, head_size)
    scores = jnp.einsum(
        "ighd,khd->hgik", queries, all_keys, preferred_element_type=jnp.float32
    ) / jnp.sqrt(jnp.float32(head_size))
    cols = jnp.arange(total_keys, dtype=jnp.int32)[None, :]
    rows = jnp.arange(resp_rows, dtype=jnp.int32)[:, None]
    allowed = jnp.where(cols < slot_len, cols < plen, cols - slot_len <= rows)
    scores = jnp.where(allowed[None, None], scores, -jnp.inf)
    top = jnp.max(scores, axis=-1, keepdims=True)
    expo = jnp.exp(scores - top)
    probs = (expo / jnp.sum(expo, axis=-1, keepdims=True)).astype(jnp.bfloat16)
    out = jnp.einsum("hgik,khd->ighd", probs, all_vals, preferred_element_type=jnp.float32)
    out = out.reshape(resp_rows, query_heads * head_size)
    live = jnp.arange(resp_rows, dtype=jnp.int32)[:, None] < resp_len[0]
    return jnp.where(live, out, 0.0).astype(jnp.bfloat16)


def solution(mesh):
    in_specs = (
        P(("dp", "fsdp"), None),
        P(("dp", "fsdp"), None),
        P(("dp", "fsdp"), None),
        P(),
        P(),
        P(("dp", "fsdp"), None),
        P("dp"),
        P(("dp", "fsdp")),
        P(("dp", "fsdp")),
    )
    out_specs = P(("dp", "fsdp"), None)
    return jax.shard_map(body, mesh=mesh, in_specs=in_specs, out_specs=out_specs, check_vma=False)
```

profile of v0, /device:TPU:1, one launch (start us, length us, event | category | flops | bytes accessed | tf_op | source)
XLA Modules:
  0.0 307.9 jit_solution(2712573422227953853)
XLA Ops:
  6.5 0.0 all-gather.3.cloned.1.call-start
  6.5 0.7 all-gather.3.cloned.1.call-update
  7.3 0.0 all-gather.5.cloned.1.call-start
  8.0 1.2 dynamic_slice.7
  9.7 1.8 fusion.2
  11.5 0.1 pad_maximum_fusion.6
  11.6 0.4 multiply_cosine_fusion
  12.0 0.0 copy-start.1
  12.0 217.3 %all-gather.3.cloned.1.call-done = bf16[4096,1024]{1,0:T(8,128)(2,1)} async-done(((bf16[8,1024]{1,0:T(8,128)(2,1)}), bf16[4096,1024]{1,0:T(8,128)(2,1)}) %all-gather.3.cloned.1.call-update) | async-done | bytes 8388624 | tf_op jit(solution)/shard_map/all_gather | solution.py:42
  229.3 5.7 %fusion.25 = (bf16[192,1024]{1,0:T(8,128)(2,1)S(1)}, f32[192,1024]{1,0:T(8,128)S(1)}) fusion(bf16[4096,1024]{1,0:T(8,128)(2,1)} %all-gather.3.cloned.1.call-done, f32[4096]{0:T(1024)} %param.12, f32[192]{0:T(256)S(1)} %add_rsqrt_fusion.1, bf16[128,4096]{1,0:T(8,128)(2,1)} %param.10, bf16[64,4096]{1,0:T(8,128)(2,1)} %param.9), kind=kOutput, calls=%fused_computation.57 | convolution fusion | flops 1616314368 | bytes 11158272 | tf_op jit(solution)/shard_map/dot_general | solution.py:40
  235.1 0.0 copy-start
  235.1 0.1 reshape.168
  235.3 0.3 multiply_reduce_fusion
  235.6 0.0 copy-done.1
  235.6 0.3 multiply_multiply_fusion
  235.9 0.4 subtract_convert_fusion
  236.3 0.3 pad_maximum_fusion.4
  236.6 0.7 pad_maximum_fusion.5
  237.3 0.0 all-gather.5.cloned.1.call-update
  237.3 0.0 copy-done
  237.3 0.4 reshape.174
  238.3 0.5 iota_compare_fusion.1
  238.9 0.3 fusion.17
  239.2 0.2 fusion.18
  239.5 54.4 %all-gather.5.cloned.1.call-done = bf16[2048,1024]{1,0:T(8,128)(2,1)} async-done(((bf16[64,1024]{1,0:T(8,128)(2,1)}), bf16[2048,1024]{1,0:T(8,128)(2,1)}) %all-gather.5.cloned.1.call-update) | async-done | bytes 4194320 | tf_op jit(solution)/shard_map/all_gather | solution.py:59
  293.8 1.3 constant_dynamic-slice_fusion
  295.1 0.1 fusion.24
  295.2 0.1 pad_maximum_fusion.2
  295.3 0.3 copy.34
  295.6 0.3 copy.35
  295.9 0.9 fusion.15
  296.8 2.4 fusion.26
  299.2 0.6 fusion.13
  299.9 0.1 fusion.14
  300.0 1.0 copy.40
  (13 shorter events, 0.2 us)
Async XLA Ops:
  6.5 222.8 %all-gather.3.cloned.1.call-start = ((), (), s32[]{:S(2)}) async-start(), calls=%async_computation | async-start | bytes 8404992 | tf_op jit(solution)/shard_map/all_gather | solution.py:42
  7.3 286.6 %all-gather.5.cloned.1.call-start = ((), (), s32[]{:S(2)}) async-start(), calls=%async_computation.1 | async-start | bytes 4325376 | tf_op jit(solution)/shard_map/all_gather | solution.py:59
  12.0 223.6 %copy-start.1 = (f32[128]{0:T(128)S(1)}, f32[128]{0:T(128)}, u32[]{:S(2)}) copy-start(f32[128]{0:T(128)} %param.13) | copy-start | bytes 1540
  235.1 2.2 copy-start
Sparse Core Ops, SparseCore 0:
  11.9 217.3 all-gather.2
  237.4 56.3 all-gather.4
where the time goes:
time: 308 us
  waiting for transfers between devices  272 us (88%)
  between operations  15.5 us (5%)
  other arithmetic  7.83 us (3%)
  matrix products  7.23 us (2%)
  local copies, waits for them, and re-layouts  4.85 us (2%)
    all_gather x1, waiting for transfers between devices, body(): lax.all_gather(w_kv, ('dp', 'fsdp'), axis=0, tiled=True)  217 us
    all_gather x1, waiting for transfers between devices, body(): gathered = lax.all_gather(prompt_cache, 'fsdp', axis=0, tiled=True)  54.4 us
  transfers between devices with their start and end apart: 2, of which 2 were waited for; matrix products, arithmetic and copies ran while one was open for 2% of the time, Pallas kernels for 0%

commit v1 on v0

v1 whole, which is shorter than its diff:
```python
import functools

import jax
import jax.numpy as jnp
import numpy as np
from jax import lax
from jax.experimental import pallas as pl
from jax.experimental.pallas import tpu as pltpu
from jax.sharding import PartitionSpec as P

MESH = pl.DeviceIdType.MESH
NZ, NX, NY = 16, 4, 4
HD = 128
KVH = 4
QPK = 4
LP = 512
LR = 128
PG = 4
SUB = 16
D = 4096
EPS = 1e-06
BIG = -1e30


def place():
    f = lax.axis_index("fsdp")
    return lax.axis_index("dp"), f // 8, (f // 2) % NY, f % 2


def device(z, x, y, c):
    return (z, (x * NY + y) * 2 + c)


def gather_kernel(
    prompt_ref, resp_ref, w_ref, gain_ref, key_gain_ref, freq_ref, len_ref, owner_ref,
    out_ref,
    hid, normed, wall, wrx, wbuf, acc, meta, meta_rx, cos_ref, sin_ref, cache, picked,
    in_sem, ex_send, ex_recv, z_send, z_recv,
    w2_send, w2_recv, w3_send, w3_recv, w4_send, w4_recv,
    p2_send, p2_recv, p3_send, p3_recv, p4_send, p4_recv,
):
    z, x, y, c = place()
    other = 1 - c

    def to_z(d):
        return device((z + d) % NZ, x, y, c)

    def to_x(d):
        return device(z, (x + d) % NX, y, c)

    def to_y(d):
        return device(z, x, (y + d) % NY, c)

    mate = device(z, x, y, other)

    def copy(src, dst, send, recv, to):
        return pltpu.make_async_remote_copy(
            src_ref=src, dst_ref=dst, send_sem=send, recv_sem=recv, device_id=to, device_id_type=MESH
        )

    in_copies = [
        pltpu.make_async_copy(prompt_ref, hid.at[pl.ds(0, PG)], in_sem.at[0]),
        pltpu.make_async_copy(resp_ref, hid.at[pl.ds(PG, 8)], in_sem.at[1]),
    ]
    for cp in in_copies:
        cp.start()

    peers = [mate] + [to_z(d) for d in range(1, NZ)] + [to_x(d) for d in (1, 2, 3)] + [to_y(d) for d in (1, 2, 3)]
    barrier = pltpu.get_barrier_semaphore()
    for peer in peers:
        pl.semaphore_signal(barrier, inc=1, device_id=peer, device_id_type=MESH)

    for kv in range(2):
        for h in range(KVH):
            j = kv * KVH + h
            wall[kv, h] = w_ref[:, j * HD : (j + 1) * HD].astype(jnp.float32)
    owner = owner_ref[0]
    plen = len_ref[owner].astype(jnp.float32)
    line = lax.broadcasted_iota(jnp.int32, (8, HD), 0)
    meta[...] = jnp.where(line == 0, plen, jnp.where(line - 1 == owner, 1.0, 0.0))
    pl.semaphore_wait(barrier, len(peers))

    ex_w = copy(wall.at[:, pl.ds(2 * other, 2)], wrx, ex_send.at[0], ex_recv.at[0], mate)
    ex_w.start()
    ex_m = copy(meta, meta_rx, ex_send.at[1], ex_recv.at[1], mate)
    ex_m.start()
    ex_w.wait_recv()
    for kv in range(2):
        for h in range(2):
            mine = wall[kv, 2 * c + h]
            theirs = wrx[kv, h]
            first = jnp.where(c == 0, mine, theirs)
            second = jnp.where(c == 0, theirs, mine)
            wbuf[2 * kv + h, z, x, y] = jnp.concatenate([first, second], axis=0).astype(jnp.bfloat16)

    def z_copy(d):
        block = wbuf.at[:, z, x, y]
        return copy(block, block, z_send.at[d], z_recv.at[d], to_z(d))

    for d in (1, 15, 2, 14, 3, 13, 4, 12, 5, 11, 6, 10, 7, 9, 8):
        z_copy(d).start()

    for cp in in_copies:
        cp.wait()
    gain = gain_ref[...]

    @pl.loop(0, 12)
    def _(i):
        v = hid[i].astype(jnp.float32)
        scale = lax.rsqrt(jnp.mean(v * v, axis=-1, keepdims=True) + EPS)
        row = jnp.where(i < PG, 2 * i + c, 2 * PG + 8 * c + i - PG)
        normed[row] = (v * scale * gain).astype(jnp.bfloat16)

    ex_n = []
    for p in range(PG):
        rows = normed.at[2 * p + c]
        ex_n.append(copy(rows, rows, ex_send.at[2 + p], ex_recv.at[2 + p], mate))
    rows = normed.at[pl.ds(2 * PG + 8 * c, 8)]
    ex_n.append(copy(rows, rows, ex_send.at[6], ex_recv.at[6], mate))
    for cp in ex_n:
        cp.start()

    ex_m.wait_recv()
    freq = freq_ref[...]
    lane = lax.broadcasted_iota(jnp.int32, (32, HD), 1)
    row = lax.broadcasted_iota(jnp.int32, (32, HD), 0)
    sign = jnp.where(lane < HD // 2, -1.0, 1.0)
    mine, theirs = meta[0:1, :], meta_rx[0:1, :]
    lens = (jnp.where(c == 0, mine, theirs), jnp.where(c == 0, theirs, mine))

    @pl.loop(0, 9)
    def _(i):
        j = i - 1
        base = jnp.where(i == 0, (32 * (x * NY + y)).astype(jnp.float32), jnp.where(j < 4, lens[0], lens[1]))
        off = jnp.where(i == 0, 0, (j % 4) * 32)
        angle = (base + (row + off).astype(jnp.float32)) * freq
        cos_ref[i] = jnp.cos(angle)
        sin_ref[i] = jnp.sin(angle) * sign

    acc[...] = jnp.zeros_like(acc)
    for cp in ex_n:
        cp.wait_recv()

    def order(t):
        step = jnp.where(t % 2 == 1, (t + 1) // 2, (8 - t // 2) % 8)
        return (z // 2 + step) % 8

    def planes(t):
        ph = order(t)
        return 2 * ph, 2 * ph + 1

    def w2_copies(t):
        za, zb = planes(t)
        a, b = wbuf.at[:, za, x, y], wbuf.at[:, zb, x, y]
        out = []
        for d in (1, 3, 2):
            out.append(copy(a, a, w2_send.at[t, d - 1], w2_recv.at[t, d - 1], to_y(d)))
            out.append(copy(b, b, w2_send.at[t, d + 2], w2_recv.at[t, d + 2], to_x(d)))
        return out

    def w3_copies(t):
        za, zb = planes(t)
        a, b = wbuf.at[:, za, x], wbuf.at[:, zb, :, y]
        return [
            copy(a, a, w3_send.at[t, 0], w3_recv.at[t, 0], to_x(1)),
            copy(b, b, w3_send.at[t, 1], w3_recv.at[t, 1], to_y(1)),
            copy(a, a, w3_send.at[t, 2], w3_recv.at[t, 2], to_x(3)),
            copy(b, b, w3_send.at[t, 3], w3_recv.at[t, 3], to_y(3)),
        ]

    def w4_copies(t):
        za, zb = planes(t)
        lo, hi = pl.ds(0, 2), pl.ds(2, 2)
        a0, b0 = wbuf.at[lo, za, (x + 3) % NX], wbuf.at[lo, zb, :, (y + 3) % NY]
        a1, b1 = wbuf.at[hi, za, (x + 1) % NX], wbuf.at[hi, zb, :, (y + 1) % NY]
        return [
            copy(a0, a0, w4_send.at[t, 0], w4_recv.at[t, 0], to_x(1)),
            copy(b0, b0, w4_send.at[t, 1], w4_recv.at[t, 1], to_y(1)),
            copy(a1, a1, w4_send.at[t, 2], w4_recv.at[t, 2], to_x(3)),
            copy(b1, b1, w4_send.at[t, 3], w4_recv.at[t, 3], to_y(3)),
        ]

    def wait_z(plane):
        d = (z - plane + NZ) % NZ
        block = wbuf.at[:, plane, x, y]
        copy(block, block, z_send.at[d], z_recv.at[d], mate).wait_recv()

    @pl.loop(0, 11)
    def _(t):
        @pl.when(jnp.logical_and(t >= 2, t < 10))
        def _():
            s = t - 2
            for cp in w3_copies(s):
                cp.wait_recv()
            for cp in w4_copies(s):
                cp.start()

        @pl.when(jnp.logical_and(t >= 1, t < 9))
        def _():
            s = t - 1
            for cp in w2_copies(s):
                cp.wait_recv()
            for cp in w3_copies(s):
                cp.start()

        @pl.when(t < 8)
        def _():
            za, zb = planes(t)

            @pl.when(za != z)
            def _():
                wait_z(za)

            @pl.when(zb != z)
            def _():
                wait_z(zb)

            for cp in w2_copies(t):
                cp.start()

        @pl.when(t >= 3)
        def _():
            s = t - 3
            for cp in w4_copies(s):
                cp.wait_recv()
            ph = order(s)
            za = 2 * ph
            parts = [wbuf[u, pl.ds(za, 2)].reshape(512, HD) for u in range(4)]
            w = jnp.concatenate(parts, axis=1)
            left = normed[:, :, pl.ds(pl.multiple_of(ph * 512, 512), 512)].reshape(384, 512)
            acc[...] += jnp.dot(left, w, preferred_element_type=jnp.float32)

    key_gain = key_gain_ref[...]

    def finish(kv, h, start, size, cos, sin):
        j = kv * 2 + h
        v = acc[start : start + size, j * HD : (j + 1) * HD]
        if kv == 0:
            v = v * lax.rsqrt(jnp.mean(v * v, axis=-1, keepdims=True) + EPS) * key_gain
            v = v * cos + pltpu.roll(v, HD // 2, 1) * sin
        return v.astype(jnp.bfloat16)

    for h in range(2):
        for kv in range(2):
            for p in range(PG):
                cache[h, kv, p, x, y] = finish(kv, h, p * 32, 32, cos_ref[0], sin_ref[0])

    def p2_copies(p):
        a, b = cache.at[0, :, p, x, y], cache.at[1, :, p, x, y]
        out = []
        for d in (1, 3, 2):
            out.append(copy(a, a, p2_send.at[p, d - 1], p2_recv.at[p, d - 1], to_x(d)))
            out.append(copy(b, b, p2_send.at[p, d + 2], p2_recv.at[p, d + 2], to_y(d)))
        return out

    def p3_copies(p):
        a, b = cache.at[0, :, p, :, y], cache.at[1, :, p, x]
        return [
            copy(a, a, p3_send.at[p, 0], p3_recv.at[p, 0], to_y(1)),
            copy(b, b, p3_send.at[p, 1], p3_recv.at[p, 1], to_x(1)),
            copy(a, a, p3_send.at[p, 2], p3_recv.at[p, 2], to_y(3)),
            copy(b, b, p3_send.at[p, 3], p3_recv.at[p, 3], to_x(3)),
        ]

    def p4_copies(p):
        a0, b0 = cache.at[0, 0, p, :, (y + 3) % NY], cache.at[1, 0, p, (x + 3) % NX]
        a1, b1 = cache.at[0, 1, p, :, (y + 1) % NY], cache.at[1, 1, p, (x + 1) % NX]
        return [
            copy(a0, a0, p4_send.at[p, 0], p4_recv.at[p, 0], to_y(1)),
            copy(b0, b0, p4_send.at[p, 1], p4_recv.at[p, 1], to_x(1)),
            copy(a1, a1, p4_send.at[p, 2], p4_recv.at[p, 2], to_y(3)),
            copy(b1, b1, p4_send.at[p, 3], p4_recv.at[p, 3], to_x(3)),
        ]

    for p in range(PG):
        for cp in p2_copies(p):
            cp.start()

    def resp(kv, h, which):
        cos = cos_ref[pl.ds(1 + 4 * which, 4)].reshape(LR, HD)
        sin = sin_ref[pl.ds(1 + 4 * which, 4)].reshape(LR, HD)
        j = kv * 2 + h
        v = acc[pl.ds(pl.multiple_of(128 + 128 * which, 128), LR), j * HD : (j + 1) * HD]
        if kv == 0:
            v = v * lax.rsqrt(jnp.mean(v * v, axis=-1, keepdims=True) + EPS) * key_gain
            v = v * cos + pltpu.roll(v, HD // 2, 1) * sin
        return v.astype(jnp.bfloat16)

    for h in range(2):
        for kv in range(2):
            picked[kv, h, LP : LP + LR] = resp(kv, h, other)
            out_ref[kv, 2 * c + h, LP : LP + LR] = resp(kv, h, c)

    @pl.loop(0, PG + 2)
    def _(t):
        @pl.when(jnp.logical_and(t >= 1, t < PG + 1))
        def _():
            p = t - 1
            for cp in p3_copies(p):
                cp.wait_recv()
            for cp in p4_copies(p):
                cp.start()

        @pl.when(t < PG)
        def _():
            for cp in p2_copies(t):
                cp.wait_recv()
            for cp in p3_copies(t):
                cp.start()

        @pl.when(t >= 2)
        def _():
            for cp in p4_copies(t - 2):
                cp.wait_recv()

    for h in range(2):
        for kv in range(2):
            total = None
            for p in range(PG):
                weight = meta_rx[1 + p : 2 + p, :].astype(jnp.bfloat16)
                part = cache[h, kv, p].reshape(LP, HD) * weight
                total = part if total is None else total + part
            picked[kv, h, 0:LP] = total
    block = out_ref.at[:, pl.ds(2 * c, 2)]
    ex_o = copy(picked, block, ex_send.at[7], ex_recv.at[7], mate)
    ex_o.start()
    for h in range(2):
        for kv in range(2):
            out_ref[kv, 2 * c + h, 0:LP] = cache[h, kv, owner].reshape(LP, HD)
    ex_o.wait_recv()

    ex_w.wait_send()
    ex_m.wait_send()
    ex_o.wait_send()
    for cp in ex_n:
        cp.wait_send()
    for d in range(1, NZ):
        z_copy(d).wait_send()

    @pl.loop(0, 8)
    def _(t):
        for cp in w2_copies(t) + w3_copies(t) + w4_copies(t):
            cp.wait_send()

    @pl.loop(0, PG)
    def _(p):
        for cp in p2_copies(p) + p3_copies(p) + p4_copies(p):
            cp.wait_send()


def attend_kernel(len_ref, owner_ref, rlen_ref, q_ref, kv_ref, o_ref):
    scale = np.float32(np.log2(np.e) / np.sqrt(HD))
    head = pl.program_id(0)

    def columns(g):
        return pl.ds(pl.multiple_of((g * KVH + head) * HD, HD), HD)

    q = jnp.concatenate([q_ref[:, columns(g)] for g in range(QPK)], axis=0)
    keys, vals = kv_ref[0, 0], kv_ref[1, 0]
    s = lax.dot_general(q, keys, (((1,), (1,)), ((), ())), preferred_element_type=jnp.float32) * scale
    plen = len_ref[owner_ref[0]]
    cols = lax.broadcasted_iota(jnp.int32, (LR, LP + LR), 1)
    rows = lax.broadcasted_iota(jnp.int32, (LR, LP + LR), 0)
    allowed = cols < jnp.where(cols < LP, plen, LP + 1 + rows)
    bias = jnp.where(allowed, 0.0, BIG)
    live = lax.broadcasted_iota(jnp.int32, (LR, HD), 0) < rlen_ref[0]
    for g in range(QPK):
        t = s[g * LR : (g + 1) * LR] + bias
        e = jnp.exp2(t - jnp.max(t, axis=-1, keepdims=True))
        total = jnp.sum(e, axis=-1, keepdims=True)
        out = jnp.dot(e.astype(jnp.bfloat16), vals, preferred_element_type=jnp.float32) / total
        o_ref[:, columns(g)] = jnp.where(live, out, 0.0).astype(jnp.bfloat16)


def body(
    prompt_hidden, resp_hidden, resp_query, ln_gain, key_gain, w_kv, prompt_len, resp_len, owner
):
    half = HD // 2
    inv = np.float32(1000000.0) ** (-(np.arange(half, dtype=np.float32) * np.float32(2.0)) / np.float32(HD))
    freq = jnp.asarray(np.concatenate([inv, inv])[None, :].astype(np.float32))
    vmem = pl.BlockSpec(memory_space=pltpu.VMEM)
    smem = pl.BlockSpec(memory_space=pltpu.SMEM)
    anym = pl.BlockSpec(memory_space=pl.ANY)
    bf, f32 = jnp.bfloat16, jnp.float32
    dma = pltpu.SemaphoreType.DMA
    kv = pl.pallas_call(
        gather_kernel,
        name="project_and_share",
        out_shape=jax.ShapeDtypeStruct((2, KVH, LP + LR, HD), bf),
        in_specs=[anym, anym, vmem, vmem, vmem, vmem, smem, smem],
        out_specs=vmem,
        scratch_shapes=[
            pltpu.VMEM((12, SUB, D), bf),
            pltpu.VMEM((24, SUB, D), bf),
            pltpu.VMEM((2, KVH, 8, HD), f32),
            pltpu.VMEM((2, 2, 8, HD), f32),
            pltpu.VMEM((4, NZ, NX, NY, SUB, HD), bf),
            pltpu.VMEM((384, 512), f32),
            pltpu.VMEM((8, HD), f32),
            pltpu.VMEM((8, HD), f32),
            pltpu.VMEM((9, 32, HD), f32),
            pltpu.VMEM((9, 32, HD), f32),
            pltpu.VMEM((2, 2, PG, NX, NY, 32, HD), bf),
            pltpu.VMEM((2, 2, LP + LR, HD), bf),
            dma((2,)), dma((8,)), dma((8,)), dma((NZ,)), dma((NZ,)),
            dma((8, 6)), dma((8, 6)), dma((8, 4)), dma((8, 4)), dma((8, 4)), dma((8, 4)),
            dma((PG, 6)), dma((PG, 6)), dma((PG, 4)), dma((PG, 4)), dma((PG, 4)), dma((PG, 4)),
        ],
        compiler_params=pltpu.CompilerParams(
            collective_id=0, has_side_effects=True, vmem_limit_bytes=48 << 20
        ),
    )(
        prompt_hidden.reshape(PG, SUB, D), resp_hidden.reshape(8, SUB, D), w_kv,
        ln_gain.reshape(1, D), key_gain.reshape(1, HD), freq, prompt_len, owner,
    )
    return pl.pallas_call(
        attend_kernel,
        name="attend",
        out_shape=jax.ShapeDtypeStruct((LR, KVH * QPK * HD), bf),
        grid=(KVH,),
        in_specs=[
            smem, smem, smem,
            pl.BlockSpec((LR, KVH * QPK * HD), lambda h: (0, 0)),
            pl.BlockSpec((2, 1, LP + LR, HD), lambda h: (0, h, 0, 0)),
        ],
        out_specs=pl.BlockSpec((LR, KVH * QPK * HD), lambda h: (0, 0)),
        compiler_params=pltpu.CompilerParams(vmem_limit_bytes=32 << 20),
    )(prompt_len, owner, resp_len, resp_query, kv)


def solution(mesh):
    in_specs = (
        P(("dp", "fsdp"), None),
        P(("dp", "fsdp"), None),
        P(("dp", "fsdp"), None),
        P(),
        P(),
        P(("dp", "fsdp"), None),
        P("dp"),
        P(("dp", "fsdp")),
        P(("dp", "fsdp")),
    )
    out_specs = P(("dp", "fsdp"), None)
    return jax.shard_map(body, mesh=mesh, in_specs=in_specs, out_specs=out_specs, check_vma=False)
```

time: 308 us -> 113 us (0.37)
  waiting for transfers between devices: 272 us -> 0 us
  Pallas kernels: 0 us -> 106 us
  between operations: 15.5 us -> 1.33 us
  other arithmetic: 7.83 us -> 0 us
  matrix products: 7.23 us -> 0 us
    all_gather x2 -> x0, waiting for transfers between devices: 272 us -> none  [the longest x1 217 us: body(): lax.all_gather(w_kv, ('dp', 'fsdp'), axis=0, tiled=True)]
    pallas_call x0 -> x2, Pallas kernels: none -> 106 us  [the longest x1 101 us: body(): pl.pallas_call(gather_kernel, name='project_and_share', out_shape=jax.Sha...]
    dot_general x3 -> x0, matrix products: 7.23 us -> none  [the longest x1 5.73 us: body(): jnp.dot(normed, lax.all_gather(w_kv, ('dp', 'fsdp'), axis=0, tiled=True),...]
    unnamed x6 -> x16, local copies, waits for them, and re-layouts: 0.06 us -> 5.66 us
  transfers between devices with their start and end apart: 2 -> 0, of which waited for: 2 -> 0; matrix products, arithmetic and copies ran while one was open for 2% -> 0% of each run, Pallas kernels for 0% -> 0%
where the time goes in v1:
time: 113 us
  Pallas kernels  106 us (94%)
  local copies, waits for them, and re-layouts  5.66 us (5%)
  between operations  1.33 us (1%)
    pallas_call x1, Pallas kernels, body(): pl.pallas_call(gather_kernel, name='project_and_share', out_shape=jax.Sha...  101 us
    unnamed x16, local copies, waits for them, and re-layouts  5.66 us
    pallas_call x1, Pallas kernels, body(): pl.pallas_call(attend_kernel, name='attend', out_shape=jax.ShapeDtypeStru...  4.58 us

profile of v1, /device:TPU:1, one launch (start us, length us, event | category | flops | bytes accessed | tf_op | source)
XLA Modules:
  0.0 113.0 jit_solution(903841053006632638)
XLA Ops:
  1.3 0.0 copy-start
  1.3 1.2 %copy-done = bf16[128,4096]{1,0:T(8,128)(2,1)S(1)} copy-done((bf16[128,4096]{1,0:T(8,128)(2,1)S(1)}, bf16[128,4096]{1,0:T(8,128)(2,1)}, u32[]{:S(2)}) %copy-start) | copy-done | bytes 1048600
  2.5 0.0 copy-start.1
  2.5 1.0 copy-done.1
  3.6 0.0 copy-start.3
  3.6 0.7 copy-done.3
  4.3 0.0 copy-start.4
  4.3 0.7 copy-done.4
  5.0 0.0 copy-start.5
  5.0 0.7 copy-done.5
  5.7 0.0 copy-start.6
  5.7 0.7 copy-done.6
  6.3 0.0 copy-start.7
  6.3 0.7 copy-done.7
  7.0 0.0 copy-start.2
  7.0 101.4 %project_and_share.1.kv_ref = bf16[2,4,640,128]{3,2,1,0:T(8,128)(2,1)S(1)} custom-call(bf16[4,16,4096]{2,1,0:T(8,128)(2,1)S(1)} %bitcast.5, bf16[8,16,4096]{2,1,0:T(8,128)(2,1)S(1)} %bitcast.4, bf16[8,1024]{1,0:T(8,128)(2,1)S(1)} %copy-done.3, f32[1,4096]{1,0:T(1,128)S(1)} %bitcast.6, f32[1,128]{1,0:T(1,128)S(1)} %bitcast.7, f32[1,128]{1,0:T(1,128)S(1)} %copy-done.7, ...), custom_call_target="tpu_custom_call" | custom-call | tf_op jit(solution)/shard_map/project_and_share/pallas_call | solution.py:386
  108.4 0.0 copy-done.2
  108.4 4.6 %attend.1 = bf16[128,2048]{1,0:T(8,128)(2,1)} custom-call(s32[4]{0:T(128)S(1)} %copy-done.5, s32[1]{0:T(128)S(6)} %copy.12.owner_ref, s32[1]{0:T(128)S(6)} %copy.11.rlen_ref, bf16[128,2048]{1,0:T(8,128)(2,1)S(1)} %copy-done.2, bf16[2,4,640,128]{3,2,1,0:T(8,128)(2,1)S(1)} %project_and_share.1.kv_ref), custom_call_target="tpu_custom_call" | custom-call | tf_op jit(solution)/shard_map/attend/pallas_call | solution.py:416
Async XLA Ops:
  1.3 1.2 %copy-start = (bf16[128,4096]{1,0:T(8,128)(2,1)S(1)}, bf16[128,4096]{1,0:T(8,128)(2,1)}, u32[]{:S(2)}) copy-start(bf16[128,4096]{1,0:T(8,128)(2,1)} %param.11) | copy-start | bytes 3145732
  2.5 1.0 copy-start.1
  3.6 0.7 copy-start.3
  4.3 0.7 copy-start.4
  5.0 0.7 copy-start.5
  5.7 0.7 copy-start.6
  6.3 0.7 copy-start.7
  7.0 101.4 %copy-start.2 = (bf16[128,2048]{1,0:T(8,128)(2,1)S(1)}, bf16[128,2048]{1,0:T(8,128)(2,1)}, u32[]{:S(2)}) copy-start(bf16[128,2048]{1,0:T(8,128)(2,1)} %q_ref.1) | copy-start | bytes 1572868

commit v2 on v1

--- a/solution.py
+++ b/solution.py
@@ -20,6 +20,7 @@
 D = 4096
 EPS = 1e-06
 BIG = -1e30
+LAG = 2
 
 
 def place():
@@ -32,10 +33,11 @@
 
 
 def gather_kernel(
-    prompt_ref, resp_ref, w_ref, gain_ref, key_gain_ref, freq_ref, len_ref, owner_ref,
+    prompt_ref, resp_ref, w_ref, gain_hbm, key_gain_hbm, freq_hbm, len_hbm, owner_hbm,
     out_ref,
+    gain_ref, key_gain_ref, freq_ref, len_ref, owner_ref,
     hid, normed, wall, wrx, wbuf, acc, meta, meta_rx, cos_ref, sin_ref, cache, picked,
-    in_sem, ex_send, ex_recv, z_send, z_recv,
+    in_sem, ex_send, ex_recv, n_send, n_recv, up_send, up_recv, down_send, down_recv,
     w2_send, w2_recv, w3_send, w3_recv, w4_send, w4_recv,
     p2_send, p2_recv, p3_send, p3_recv, p4_send, p4_recv,
 ):
@@ -59,13 +61,18 @@
         )
 
     in_copies = [
-        pltpu.make_async_copy(prompt_ref, hid.at[pl.ds(0, PG)], in_sem.at[0]),
-        pltpu.make_async_copy(resp_ref, hid.at[pl.ds(PG, 8)], in_sem.at[1]),
+        pltpu.make_async_copy(len_hbm, len_ref, in_sem.at[0]),
+        pltpu.make_async_copy(owner_hbm, owner_ref, in_sem.at[1]),
+        pltpu.make_async_copy(gain_hbm, gain_ref, in_sem.at[2]),
+        pltpu.make_async_copy(key_gain_hbm, key_gain_ref, in_sem.at[3]),
+        pltpu.make_async_copy(freq_hbm, freq_ref, in_sem.at[4]),
+        pltpu.make_async_copy(prompt_ref, hid.at[pl.ds(0, PG)], in_sem.at[5]),
+        pltpu.make_async_copy(resp_ref, hid.at[pl.ds(PG, 8)], in_sem.at[6]),
     ]
     for cp in in_copies:
         cp.start()
 
-    peers = [mate] + [to_z(d) for d in range(1, NZ)] + [to_x(d) for d in (1, 2, 3)] + [to_y(d) for d in (1, 2, 3)]
+    peers = [mate] + [to_z(1), to_z(15)] + [to_x(d) for d in (1, 2, 3)] + [to_y(d) for d in (1, 2, 3)]
     barrier = pltpu.get_barrier_semaphore()
     for peer in peers:
         pl.semaphore_signal(barrier, inc=1, device_id=peer, device_id_type=MESH)
@@ -74,6 +81,8 @@
         for h in range(KVH):
             j = kv * KVH + h
             wall[kv, h] = w_ref[:, j * HD : (j + 1) * HD].astype(jnp.float32)
+    in_copies[0].wait()
+    in_copies[1].wait()
     owner = owner_ref[0]
     plen = len_ref[owner].astype(jnp.float32)
     line = lax.broadcasted_iota(jnp.int32, (8, HD), 0)
@@ -91,35 +100,21 @@
             theirs = wrx[kv, h]
             first = jnp.where(c == 0, mine, theirs)
             second = jnp.where(c == 0, theirs, mine)
-            wbuf[2 * kv + h, z, x, y] = jnp.concatenate([first, second], axis=0).astype(jnp.bfloat16)
-
-    def z_copy(d):
-        block = wbuf.at[:, z, x, y]
-        return copy(block, block, z_send.at[d], z_recv.at[d], to_z(d))
-
-    for d in (1, 15, 2, 14, 3, 13, 4, 12, 5, 11, 6, 10, 7, 9, 8):
-        z_copy(d).start()
-
-    for cp in in_copies:
+            wbuf[z, x, y, 2 * kv + h] = jnp.concatenate([first, second], axis=0).astype(jnp.bfloat16)
+
+    def up_copy(t):
+        block = wbuf.at[(z + NZ - t) % NZ, x, y]
+        return copy(block, block, up_send.at[t], up_recv.at[t], to_z(1))
+
+    def down_copy(t):
+        block = wbuf.at[(z + t) % NZ, x, y]
+        return copy(block, block, down_send.at[t], down_recv.at[t], to_z(NZ - 1))
+
+    up_copy(0).start()
+    down_copy(0).start()
+
+    for cp in in_copies[2:]:
         cp.wait()
-    gain = gain_ref[...]
-
-    @pl.loop(0, 12)
-    def _(i):
-        v = hid[i].astype(jnp.float32)
-        scale = lax.rsqrt(jnp.mean(v * v, axis=-1, keepdims=True) + EPS)
-        row = jnp.where(i < PG, 2 * i + c, 2 * PG + 8 * c + i - PG)
-        normed[row] = (v * scale * gain).astype(jnp.bfloat16)
-
-    ex_n = []
-    for p in range(PG):
-        rows = normed.at[2 * p + c]
-        ex_n.append(copy(rows, rows, ex_send.at[2 + p], ex_recv.at[2 + p], mate))
-    rows = normed.at[pl.ds(2 * PG + 8 * c, 8)]
-    ex_n.append(copy(rows, rows, ex_send.at[6], ex_recv.at[6], mate))
-    for cp in ex_n:
-        cp.start()
-
     ex_m.wait_recv()
     freq = freq_ref[...]
     lane = lax.broadcasted_iota(jnp.int32, (32, HD), 1)
@@ -138,20 +133,27 @@
         sin_ref[i] = jnp.sin(angle) * sign
 
     acc[...] = jnp.zeros_like(acc)
-    for cp in ex_n:
-        cp.wait_recv()
-
-    def order(t):
-        step = jnp.where(t % 2 == 1, (t + 1) // 2, (8 - t // 2) % 8)
-        return (z // 2 + step) % 8
+    gain = gain_ref[...]
+
+    def norm_row(i):
+        return jnp.where(i < PG, 2 * i + c, 2 * PG + 8 * c + i - PG)
+
+    def norm_copy(i):
+        rows = normed.at[norm_row(i)]
+        return copy(rows, rows, n_send.at[i], n_recv.at[i], mate)
+
+    def norm_chunk(i):
+        v = hid[i].astype(jnp.float32)
+        scale = lax.rsqrt(jnp.mean(v * v, axis=-1, keepdims=True) + EPS)
+        normed[norm_row(i)] = (v * scale * gain).astype(jnp.bfloat16)
+        norm_copy(i).start()
 
     def planes(t):
-        ph = order(t)
-        return 2 * ph, 2 * ph + 1
+        return (z + t) % NZ, (z + 2 * NZ - 1 - t) % NZ
 
     def w2_copies(t):
         za, zb = planes(t)
-        a, b = wbuf.at[:, za, x, y], wbuf.at[:, zb, x, y]
+        a, b = wbuf.at[za, x, y], wbuf.at[zb, x, y]
         out = []
         for d in (1, 3, 2):
             out.append(copy(a, a, w2_send.at[t, d - 1], w2_recv.at[t, d - 1], to_y(d)))
@@ -160,7 +162,7 @@
 
     def w3_copies(t):
         za, zb = planes(t)
-        a, b = wbuf.at[:, za, x], wbuf.at[:, zb, :, y]
+        a, b = wbuf.at[za, x], wbuf.at[zb, :, y]
         return [
             copy(a, a, w3_send.at[t, 0], w3_recv.at[t, 0], to_x(1)),
             copy(b, b, w3_send.at[t, 1], w3_recv.at[t, 1], to_y(1)),
@@ -171,8 +173,8 @@
     def w4_copies(t):
         za, zb = planes(t)
         lo, hi = pl.ds(0, 2), pl.ds(2, 2)
-        a0, b0 = wbuf.at[lo, za, (x + 3) % NX], wbuf.at[lo, zb, :, (y + 3) % NY]
-        a1, b1 = wbuf.at[hi, za, (x + 1) % NX], wbuf.at[hi, zb, :, (y + 1) % NY]
+        a0, b0 = wbuf.at[za, (x + 3) % NX, lo], wbuf.at[zb, lo, (y + 3) % NY]
+        a1, b1 = wbuf.at[za, (x + 1) % NX, hi], wbuf.at[zb, hi, (y + 1) % NY]
         return [
             copy(a0, a0, w4_send.at[t, 0], w4_recv.at[t, 0], to_x(1)),
             copy(b0, b0, w4_send.at[t, 1], w4_recv.at[t, 1], to_y(1)),
@@ -180,24 +182,19 @@
             copy(b1, b1, w4_send.at[t, 3], w4_recv.at[t, 3], to_y(3)),
         ]
 
-    def wait_z(plane):
-        d = (z - plane + NZ) % NZ
-        block = wbuf.at[:, plane, x, y]
-        copy(block, block, z_send.at[d], z_recv.at[d], mate).wait_recv()
-
-    @pl.loop(0, 11)
+    @pl.loop(0, 8 + 3 * LAG)
     def _(t):
-        @pl.when(jnp.logical_and(t >= 2, t < 10))
-        def _():
-            s = t - 2
+        @pl.when(jnp.logical_and(t >= 2 * LAG, t < 8 + 2 * LAG))
+        def _():
+            s = t - 2 * LAG
             for cp in w3_copies(s):
                 cp.wait_recv()
             for cp in w4_copies(s):
                 cp.start()
 
-        @pl.when(jnp.logical_and(t >= 1, t < 9))
-        def _():
-            s = t - 1
+        @pl.when(jnp.logical_and(t >= LAG, t < 8 + LAG))
+        def _():
+            s = t - LAG
             for cp in w2_copies(s):
                 cp.wait_recv()
             for cp in w3_copies(s):
@@ -205,30 +202,45 @@
 
         @pl.when(t < 8)
         def _():
-            za, zb = planes(t)
-
-            @pl.when(za != z)
+            @pl.when(t >= 1)
             def _():
-                wait_z(za)
-
-            @pl.when(zb != z)
+                down_copy(t - 1).wait_recv()
+
+                @pl.when(t < 7)
+                def _():
+                    down_copy(t).start()
+
+            up_copy(t).wait_recv()
+
+            @pl.when(t < 7)
             def _():
-                wait_z(zb)
+                up_copy(t + 1).start()
 
             for cp in w2_copies(t):
                 cp.start()
 
-        @pl.when(t >= 3)
-        def _():
-            s = t - 3
+        @pl.when(t < 6)
+        def _():
+            norm_chunk(2 * t)
+            norm_chunk(2 * t + 1)
+
+        @pl.when(t == 3 * LAG)
+        def _():
+            @pl.loop(0, 12)
+            def _(i):
+                norm_copy(i).wait_recv()
+
+        @pl.when(t >= 3 * LAG)
+        def _():
+            s = t - 3 * LAG
             for cp in w4_copies(s):
                 cp.wait_recv()
-            ph = order(s)
-            za = 2 * ph
-            parts = [wbuf[u, pl.ds(za, 2)].reshape(512, HD) for u in range(4)]
-            w = jnp.concatenate(parts, axis=1)
-            left = normed[:, :, pl.ds(pl.multiple_of(ph * 512, 512), 512)].reshape(384, 512)
-            acc[...] += jnp.dot(left, w, preferred_element_type=jnp.float32)
+            left, right = [], []
+            for plane in planes(s):
+                right.append(jnp.concatenate([wbuf[plane, :, :, u].reshape(256, HD) for u in range(4)], axis=1))
+                left.append(normed[:, :, pl.ds(pl.multiple_of(plane * 256, 256), 256)].reshape(384, 256))
+            left, right = jnp.concatenate(left, axis=1), jnp.concatenate(right, axis=0)
+            acc[...] += jnp.dot(left, right, preferred_element_type=jnp.float32)
 
     key_gain = key_gain_ref[...]
 
@@ -243,10 +255,10 @@
     for h in range(2):
         for kv in range(2):
             for p in range(PG):
-                cache[h, kv, p, x, y] = finish(kv, h, p * 32, 32, cos_ref[0], sin_ref[0])
+                cache[h, p, x, y, kv] = finish(kv, h, p * 32, 32, cos_ref[0], sin_ref[0])
 
     def p2_copies(p):
-        a, b = cache.at[0, :, p, x, y], cache.at[1, :, p, x, y]
+        a, b = cache.at[0, p, x, y], cache.at[1, p, x, y]
         out = []
         for d in (1, 3, 2):
             out.append(copy(a, a, p2_send.at[p, d - 1], p2_recv.at[p, d - 1], to_x(d)))
@@ -254,7 +266,7 @@
         return out
 
     def p3_copies(p):
-        a, b = cache.at[0, :, p, :, y], cache.at[1, :, p, x]
+        a, b = cache.at[0, p, :, y], cache.at[1, p, x]
         return [
             copy(a, a, p3_send.at[p, 0], p3_recv.at[p, 0], to_y(1)),
             copy(b, b, p3_send.at[p, 1], p3_recv.at[p, 1], to_x(1)),
@@ -263,8 +275,9 @@
         ]
 
     def p4_copies(p):
-        a0, b0 = cache.at[0, 0, p, :, (y + 3) % NY], cache.at[1, 0, p, (x + 3) % NX]
-        a1, b1 = cache.at[0, 1, p, :, (y + 1) % NY], cache.at[1, 1, p, (x + 1) % NX]
+        lo, hi = pl.ds(0, 2), pl.ds(2, 2)
+        a0, b0 = cache.at[0, p, lo, (y + 3) % NY], cache.at[1, p, (x + 3) % NX, lo]
+        a1, b1 = cache.at[0, p, hi, (y + 1) % NY], cache.at[1, p, (x + 1) % NX, hi]
         return [
             copy(a0, a0, p4_send.at[p, 0], p4_recv.at[p, 0], to_y(1)),
             copy(b0, b0, p4_send.at[p, 1], p4_recv.at[p, 1], to_x(1)),
@@ -290,52 +303,69 @@
         for kv in range(2):
             picked[kv, h, LP : LP + LR] = resp(kv, h, other)
             out_ref[kv, 2 * c + h, LP : LP + LR] = resp(kv, h, c)
-
-    @pl.loop(0, PG + 2)
-    def _(t):
-        @pl.when(jnp.logical_and(t >= 1, t < PG + 1))
-        def _():
-            p = t - 1
-            for cp in p3_copies(p):
-                cp.wait_recv()
-            for cp in p4_copies(p):
-                cp.start()
-
-        @pl.when(t < PG)
-        def _():
-            for cp in p2_copies(t):
-                cp.wait_recv()
-            for cp in p3_copies(t):
-                cp.start()
-
-        @pl.when(t >= 2)
-        def _():
-            for cp in p4_copies(t - 2):
-                cp.wait_recv()
-
+    ex_r = copy(
+        picked.at[:, :, pl.ds(LP, LR)], out_ref.at[:, pl.ds(2 * c, 2), pl.ds(LP, LR)],
+        ex_send.at[2], ex_recv.at[2], mate,
+    )
+    ex_r.start()
+
+    @pl.loop(0, PG)
+    def _(p):
+        for cp in p2_copies(p):
+            cp.wait_recv()
+        for cp in p3_copies(p):
+            cp.start()
+
+    @pl.loop(0, PG)
+    def _(p):
+        for cp in p3_copies(p):
+            cp.wait_recv()
+        for cp in p4_copies(p):
+            cp.start()
+
+    @pl.loop(0, PG)
+    def _(p):
+        for cp in p4_copies(p):
+            cp.wait_recv()
+
+    ex_o = []
     for h in range(2):
         for kv in range(2):
             total = None
             for p in range(PG):
                 weight = meta_rx[1 + p : 2 + p, :].astype(jnp.bfloat16)
-                part = cache[h, kv, p].reshape(LP, HD) * weight
+                part = cache[h, p, :, :, kv].reshape(LP, HD) * weight
                 total = part if total is None else total + part
             picked[kv, h, 0:LP] = total
-    block = out_ref.at[:, pl.ds(2 * c, 2)]
-    ex_o = copy(picked, block, ex_send.at[7], ex_recv.at[7], mate)
-    ex_o.start()
+        cp = copy(
+            picked.at[:, h, pl.ds(0, LP)], out_ref.at[:, 2 * c + h, pl.ds(0, LP)],
+            ex_send.at[3 + h], ex_recv.at[3 + h], mate,
+        )
+        cp.start()
+        ex_o.append(cp)
     for h in range(2):
         for kv in range(2):
-            out_ref[kv, 2 * c + h, 0:LP] = cache[h, kv, owner].reshape(LP, HD)
-    ex_o.wait_recv()
+            out_ref[kv, 2 * c + h, 0:LP] = cache[h, owner, :, :, kv].reshape(LP, HD)
+    ex_r.wait_recv()
+    for cp in ex_o:
+        cp.wait_recv()
 
     ex_w.wait_send()
     ex_m.wait_send()
-    ex_o.wait_send()
-    for cp in ex_n:
+    ex_r.wait_send()
+    for cp in ex_o:
         cp.wait_send()
-    for d in range(1, NZ):
-        z_copy(d).wait_send()
+
+    @pl.loop(0, 12)
+    def _(i):
+        norm_copy(i).wait_send()
+
+    up_copy(7).wait_send()
+
+    @pl.loop(0, 7)
+    def _(t):
+        up_copy(t).wait_send()
+        down_copy(t).wait_send()
 
     @pl.loop(0, 8)
     def _(t):
@@ -387,27 +417,32 @@
         gather_kernel,
         name="project_and_share",
         out_shape=jax.ShapeDtypeStruct((2, KVH, LP + LR, HD), bf),
-        in_specs=[anym, anym, vmem, vmem, vmem, vmem, smem, smem],
+        in_specs=[anym, anym, vmem, anym, anym, anym, anym, anym],
         out_specs=vmem,
         scratch_shapes=[
+            pltpu.VMEM((1, D), f32),
+            pltpu.VMEM((1, HD), f32),
+            pltpu.VMEM((1, HD), f32),
+            pltpu.SMEM((PG,), jnp.int32),
+            pltpu.SMEM((1,), jnp.int32),
             pltpu.VMEM((12, SUB, D), bf),
             pltpu.VMEM((24, SUB, D), bf),
             pltpu.VMEM((2, KVH, 8, HD), f32),
             pltpu.VMEM((2, 2, 8, HD), f32),
-            pltpu.VMEM((4, NZ, NX, NY, SUB, HD), bf),
+            pltpu.VMEM((NZ, NX, NY, 4, SUB, HD), bf),
             pltpu.VMEM((384, 512), f32),
             pltpu.VMEM((8, HD), f32),
             pltpu.VMEM((8, HD), f32),
             pltpu.VMEM((9, 32, HD), f32),
             pltpu.VMEM((9, 32, HD), f32),
-            pltpu.VMEM((2, 2, PG, NX, NY, 32, HD), bf),
+            pltpu.VMEM((2, PG, NX, NY, 2, 32, HD), bf),
             pltpu.VMEM((2, 2, LP + LR, HD), bf),
-            dma((2,)), dma((8,)), dma((8,)), dma((NZ,)), dma((NZ,)),
+            dma((7,)), dma((5,)), dma((5,)), dma((12,)), dma((12,)), dma((8,)), dma((8,)), dma((7,)), dma((7,)),
             dma((8, 6)), dma((8, 6)), dma((8, 4)), dma((8, 4)), dma((8, 4)), dma((8, 4)),
             dma((PG, 6)), dma((PG, 6)), dma((PG, 4)), dma((PG, 4)), dma((PG, 4)), dma((PG, 4)),
         ],
         compiler_params=pltpu.CompilerParams(
-            collective_id=0, has_side_effects=True, vmem_limit_bytes=48 << 20
+            collective_id=0, has_side_effects=True, vmem_limit_bytes=62 << 20
         ),
     )(
         prompt_hidden.reshape(PG, SUB, D), resp_hidden.reshape(8, SUB, D), w_kv,

time: 113 us -> 80 us (0.71)
  Pallas kernels: 106 us -> 77.1 us
  local copies, waits for them, and re-layouts: 5.66 us -> 1.32 us
    pallas_call x1, Pallas kernels: 101 us -> 72.6 us  [body(): pl.pallas_call(gather_kernel, name='project_and_share', out_shape=jax.Sha...]
    unnamed x16 -> x6, local copies, waits for them, and re-layouts: 5.66 us -> 1.32 us
where the time goes in v2:
time: 80 us; the launch traced here: 79.8 us
  Pallas kernels  77.1 us (96%)
  between operations  1.35 us (2%)
  local copies, waits for them, and re-layouts  1.32 us (2%)
    pallas_call x1, Pallas kernels, body(): pl.pallas_call(gather_kernel, name='project_and_share', out_shape=jax.Sha...  72.6 us
    pallas_call x1, Pallas kernels, body(): pl.pallas_call(attend_kernel, name='attend', out_shape=jax.ShapeDtypeStru...  4.56 us

profile of v2, /device:TPU:1, one launch (start us, length us, event | category | flops | bytes accessed | tf_op | source)
XLA Modules:
  0.0 79.8 jit_solution(1425953810112577561)
XLA Ops:
  1.3 0.0 copy-start.1
  1.3 0.0 copy-start.2
  1.3 72.6 %project_and_share.1.kv_ref = bf16[2,4,640,128]{3,2,1,0:T(8,128)(2,1)} custom-call(bf16[4,16,4096]{2,1,0:T(8,128)(2,1)} %bitcast.5, bf16[8,16,4096]{2,1,0:T(8,128)(2,1)} %bitcast.4, bf16[8,1024]{1,0:T(8,128)(2,1)} %w_ref.1, f32[1,4096]{1,0:T(1,128)} %bitcast.6, f32[1,128]{1,0:T(1,128)} %bitcast.7, f32[1,128]{1,0:T(1,128)} %constant.2.clone.freq_hbm, ...), custom_call_target="tpu_custom_call" | custom-call | tf_op jit(solution)/shard_map/project_and_share/pallas_call | solution.py:416
  73.9 0.0 copy-done.1
  73.9 0.0 copy-done.2
  73.9 0.0 copy-start
  73.9 1.3 %copy-done = bf16[2,4,640,128]{3,2,1,0:T(8,128)(2,1)S(1)} copy-done((bf16[2,4,640,128]{3,2,1,0:T(8,128)(2,1)S(1)}, bf16[2,4,640,128]{3,2,1,0:T(8,128)(2,1)}, u32[]{:S(2)}) %copy-start) | copy-done | bytes 1310744
  75.2 4.6 %attend.1 = bf16[128,2048]{1,0:T(8,128)(2,1)} custom-call(s32[4]{0:T(128)S(1)} %copy-done.2, s32[1]{0:T(128)S(6)} %copy.12.owner_hbm.owner_ref, s32[1]{0:T(128)S(6)} %copy.11.rlen_ref, bf16[128,2048]{1,0:T(8,128)(2,1)S(1)} %copy-done.1, bf16[2,4,640,128]{3,2,1,0:T(8,128)(2,1)S(1)} %copy-done), custom_call_target="tpu_custom_call" | custom-call | tf_op jit(solution)/shard_map/attend/pallas_call | solution.py:451
Async XLA Ops:
  1.3 72.6 %copy-start.1 = (bf16[128,2048]{1,0:T(8,128)(2,1)S(1)}, bf16[128,2048]{1,0:T(8,128)(2,1)}, u32[]{:S(2)}) copy-start(bf16[128,2048]{1,0:T(8,128)(2,1)} %q_ref.1) | copy-start | bytes 1572868
  1.3 72.6 %copy-start.2 = (s32[4]{0:T(128)S(1)}, s32[4]{0:T(128)}, u32[]{:S(2)}) copy-start(s32[4]{0:T(128)} %len_ref.1) | copy-start | bytes 52
  73.9 1.3 %copy-start = (bf16[2,4,640,128]{3,2,1,0:T(8,128)(2,1)S(1)}, bf16[2,4,640,128]{3,2,1,0:T(8,128)(2,1)}, u32[]{:S(2)}) copy-start(bf16[2,4,640,128]{3,2,1,0:T(8,128)(2,1)} %project_and_share.1.kv_ref) | copy-start | bytes 3932164

commit v3 on v2

--- a/solution.py
+++ b/solution.py
@@ -20,7 +20,8 @@
 D = 4096
 EPS = 1e-06
 BIG = -1e30
-LAG = 2
+LAG = 4
+HOP = 3
 
 
 def place():
@@ -37,7 +38,7 @@
     out_ref,
     gain_ref, key_gain_ref, freq_ref, len_ref, owner_ref,
     hid, normed, wall, wrx, wbuf, acc, meta, meta_rx, cos_ref, sin_ref, cache, picked,
-    in_sem, ex_send, ex_recv, n_send, n_recv, up_send, up_recv, down_send, down_recv,
+    in_sem, ex_send, ex_recv, o_send, o_recv, n_send, n_recv, up_send, up_recv, down_send, down_recv,
     w2_send, w2_recv, w3_send, w3_recv, w4_send, w4_recv,
     p2_send, p2_recv, p3_send, p3_recv, p4_send, p4_recv,
 ):
@@ -72,7 +73,7 @@
     for cp in in_copies:
         cp.start()
 
-    peers = [mate] + [to_z(1), to_z(15)] + [to_x(d) for d in (1, 2, 3)] + [to_y(d) for d in (1, 2, 3)]
+    peers = [mate] + [to_z(d) for k in range(1, HOP + 1) for d in (k, NZ - k)] + [to_x(d) for d in (1, 2, 3)] + [to_y(d) for d in (1, 2, 3)]
     barrier = pltpu.get_barrier_semaphore()
     for peer in peers:
         pl.semaphore_signal(barrier, inc=1, device_id=peer, device_id_type=MESH)
@@ -102,16 +103,18 @@
             second = jnp.where(c == 0, theirs, mine)
             wbuf[z, x, y, 2 * kv + h] = jnp.concatenate([first, second], axis=0).astype(jnp.bfloat16)
 
-    def up_copy(t):
-        block = wbuf.at[(z + NZ - t) % NZ, x, y]
-        return copy(block, block, up_send.at[t], up_recv.at[t], to_z(1))
-
-    def down_copy(t):
-        block = wbuf.at[(z + t) % NZ, x, y]
-        return copy(block, block, down_send.at[t], down_recv.at[t], to_z(NZ - 1))
-
-    up_copy(0).start()
-    down_copy(0).start()
+    def up_copy(d):
+        block = wbuf.at[(z + NZ + HOP - d) % NZ, x, y]
+        return copy(block, block, up_send.at[d - 1], up_recv.at[d - 1], to_z(HOP))
+
+    def down_copy(d):
+        block = wbuf.at[(z + NZ + d - HOP) % NZ, x, y]
+        return copy(block, block, down_send.at[d - 1], down_recv.at[d - 1], to_z(NZ - HOP))
+
+    block = wbuf.at[z, x, y]
+    for d in range(1, HOP + 1):
+        copy(block, block, up_send.at[d - 1], up_recv.at[d - 1], to_z(d)).start()
+        copy(block, block, down_send.at[d - 1], down_recv.at[d - 1], to_z(NZ - d)).start()
 
     for cp in in_copies[2:]:
         cp.wait()
@@ -204,17 +207,17 @@
         def _():
             @pl.when(t >= 1)
             def _():
-                down_copy(t - 1).wait_recv()
-
-                @pl.when(t < 7)
+                down_copy(t).wait_recv()
+
+                @pl.when(t < 8 - HOP)
                 def _():
-                    down_copy(t).start()
-
-            up_copy(t).wait_recv()
-
-            @pl.when(t < 7)
+                    down_copy(t + HOP).start()
+
+            up_copy(t + 1).wait_recv()
+
+            @pl.when(t < 8 - HOP)
             def _():
-                up_copy(t + 1).start()
+                up_copy(t + 1 + HOP).start()
 
             for cp in w2_copies(t):
                 cp.start()
@@ -251,11 +254,6 @@
             v = v * lax.rsqrt(jnp.mean(v * v, axis=-1, keepdims=True) + EPS) * key_gain
             v = v * cos + pltpu.roll(v, HD // 2, 1) * sin
         return v.astype(jnp.bfloat16)
-
-    for h in range(2):
-        for kv in range(2):
-            for p in range(PG):
-                cache[h, p, x, y, kv] = finish(kv, h, p * 32, 32, cos_ref[0], sin_ref[0])
 
     def p2_copies(p):
         a, b = cache.at[0, p, x, y], cache.at[1, p, x, y]
@@ -285,8 +283,13 @@
             copy(b1, b1, p4_send.at[p, 3], p4_recv.at[p, 3], to_x(3)),
         ]
 
-    for p in range(PG):
-        for cp in p2_copies(p):
+    for s in range(4):
+        kv, cc = s // 2, s % 2
+        for h in range(2):
+            for p in range(PG):
+                cos, sin = cos_ref[0, cc * SUB : (cc + 1) * SUB], sin_ref[0, cc * SUB : (cc + 1) * SUB]
+                cache[h, s, x, y, p] = finish(kv, h, p * 32 + cc * SUB, SUB, cos, sin)
+        for cp in p2_copies(s):
             cp.start()
 
     def resp(kv, h, which):
@@ -301,10 +304,10 @@
 
     for h in range(2):
         for kv in range(2):
-            picked[kv, h, LP : LP + LR] = resp(kv, h, other)
-            out_ref[kv, 2 * c + h, LP : LP + LR] = resp(kv, h, c)
+            picked[kv, h, 16:20] = resp(kv, h, other).reshape(4, 2, SUB, HD)
+            out_ref[kv, 2 * c + h, 16:20] = resp(kv, h, c).reshape(4, 2, SUB, HD)
     ex_r = copy(
-        picked.at[:, :, pl.ds(LP, LR)], out_ref.at[:, pl.ds(2 * c, 2), pl.ds(LP, LR)],
+        picked.at[:, :, pl.ds(16, 4)], out_ref.at[:, pl.ds(2 * c, 2), pl.ds(16, 4)],
         ex_send.at[2], ex_recv.at[2], mate,
     )
     ex_r.start()
@@ -323,49 +326,48 @@
         for cp in p4_copies(p):
             cp.start()
 
-    @pl.loop(0, PG)
-    def _(p):
-        for cp in p4_copies(p):
+    def ex_copy(s):
+        kv, cc = s // 2, s % 2
+        return copy(
+            picked.at[kv, :, pl.ds(0, 16), cc], out_ref.at[kv, pl.ds(2 * c, 2), pl.ds(0, 16), cc],
+            o_send.at[s], o_recv.at[s], mate,
+        )
+
+    weights = [meta_rx[1 + p : 2 + p, :].astype(jnp.bfloat16) for p in range(PG)]
+    for s in range(4):
+        kv, cc = s // 2, s % 2
+        for cp in p4_copies(s):
             cp.wait_recv()
-
-    ex_o = []
-    for h in range(2):
-        for kv in range(2):
+        for h in range(2):
             total = None
             for p in range(PG):
-                weight = meta_rx[1 + p : 2 + p, :].astype(jnp.bfloat16)
-                part = cache[h, p, :, :, kv].reshape(LP, HD) * weight
+                part = cache[h, s, :, :, p].reshape(16, SUB, HD) * weights[p]
                 total = part if total is None else total + part
-            picked[kv, h, 0:LP] = total
-        cp = copy(
-            picked.at[:, h, pl.ds(0, LP)], out_ref.at[:, 2 * c + h, pl.ds(0, LP)],
-            ex_send.at[3 + h], ex_recv.at[3 + h], mate,
-        )
-        cp.start()
-        ex_o.append(cp)
-    for h in range(2):
-        for kv in range(2):
-            out_ref[kv, 2 * c + h, 0:LP] = cache[h, owner, :, :, kv].reshape(LP, HD)
+            picked[kv, h, 0:16, cc] = total
+        ex_copy(s).start()
+    for s in range(4):
+        for h in range(2):
+            out_ref[s // 2, 2 * c + h, 0:16, s % 2] = cache[h, s, :, :, owner].reshape(16, SUB, HD)
     ex_r.wait_recv()
-    for cp in ex_o:
-        cp.wait_recv()
+    for s in range(4):
+        ex_copy(s).wait_recv()
 
     ex_w.wait_send()
     ex_m.wait_send()
     ex_r.wait_send()
-    for cp in ex_o:
-        cp.wait_send()
+    for s in range(4):
+        ex_copy(s).wait_send()
 
     @pl.loop(0, 12)
     def _(i):
         norm_copy(i).wait_send()
 
-    up_copy(7).wait_send()
+    up_copy(8).wait_send()
 
     @pl.loop(0, 7)
     def _(t):
-        up_copy(t).wait_send()
-        down_copy(t).wait_send()
+        up_copy(t + 1).wait_send()
+        down_copy(t + 1).wait_send()
 
     @pl.loop(0, 8)
     def _(t):
@@ -380,26 +382,24 @@
 
 def attend_kernel(len_ref, owner_ref, rlen_ref, q_ref, kv_ref, o_ref):
     scale = np.float32(np.log2(np.e) / np.sqrt(HD))
-    head = pl.program_id(0)
-
-    def columns(g):
-        return pl.ds(pl.multiple_of((g * KVH + head) * HD, HD), HD)
-
-    q = jnp.concatenate([q_ref[:, columns(g)] for g in range(QPK)], axis=0)
-    keys, vals = kv_ref[0, 0], kv_ref[1, 0]
-    s = lax.dot_general(q, keys, (((1,), (1,)), ((), ())), preferred_element_type=jnp.float32) * scale
     plen = len_ref[owner_ref[0]]
     cols = lax.broadcasted_iota(jnp.int32, (LR, LP + LR), 1)
     rows = lax.broadcasted_iota(jnp.int32, (LR, LP + LR), 0)
     allowed = cols < jnp.where(cols < LP, plen, LP + 1 + rows)
     bias = jnp.where(allowed, 0.0, BIG)
     live = lax.broadcasted_iota(jnp.int32, (LR, HD), 0) < rlen_ref[0]
-    for g in range(QPK):
-        t = s[g * LR : (g + 1) * LR] + bias
-        e = jnp.exp2(t - jnp.max(t, axis=-1, keepdims=True))
-        total = jnp.sum(e, axis=-1, keepdims=True)
-        out = jnp.dot(e.astype(jnp.bfloat16), vals, preferred_element_type=jnp.float32) / total
-        o_ref[:, columns(g)] = jnp.where(live, out, 0.0).astype(jnp.bfloat16)
+    for head in range(KVH):
+        keys, vals = kv_ref[0, head], kv_ref[1, head]
+        vals = jnp.concatenate([vals, jnp.ones((LP + LR, HD), jnp.bfloat16)], axis=1)
+        for g in range(QPK):
+            at = (g * KVH + head) * HD
+            q = q_ref[:, at : at + HD]
+            s = lax.dot_general(q, keys, (((1,), (1,)), ((), ())), preferred_element_type=jnp.float32) * scale
+            t = s + bias
+            e = jnp.exp2(t - jnp.max(t, axis=-1, keepdims=True))
+            out = jnp.dot(e.astype(jnp.bfloat16), vals, preferred_element_type=jnp.float32)
+            out = out[:, :HD] / out[:, HD:]
+            o_ref[:, at : at + HD] = jnp.where(live, out, 0.0).astype(jnp.bfloat16)
 
 
 def body(
@@ -416,7 +416,7 @@
     kv = pl.pallas_call(
         gather_kernel,
         name="project_and_share",
-        out_shape=jax.ShapeDtypeStruct((2, KVH, LP + LR, HD), bf),
+        out_shape=jax.ShapeDtypeStruct((2, KVH, 20, 2, SUB, HD), bf),
         in_specs=[anym, anym, vmem, anym, anym, anym, anym, anym],
         out_specs=vmem,
         scratch_shapes=[
@@ -435,9 +435,9 @@
             pltpu.VMEM((8, HD), f32),
             pltpu.VMEM((9, 32, HD), f32),
             pltpu.VMEM((9, 32, HD), f32),
-            pltpu.VMEM((2, PG, NX, NY, 2, 32, HD), bf),
-            pltpu.VMEM((2, 2, LP + LR, HD), bf),
-            dma((7,)), dma((5,)), dma((5,)), dma((12,)), dma((12,)), dma((8,)), dma((8,)), dma((7,)), dma((7,)),
+            pltpu.VMEM((2, 4, NX, NY, PG, SUB, HD), bf),
+            pltpu.VMEM((2, 2, 20, 2, SUB, HD), bf),
+            dma((7,)), dma((3,)), dma((3,)), dma((4,)), dma((4,)), dma((12,)), dma((12,)), dma((8,)), dma((8,)), dma((7,)), dma((7,)),
             dma((8, 6)), dma((8, 6)), dma((8, 4)), dma((8, 4)), dma((8, 4)), dma((8, 4)),
             dma((PG, 6)), dma((PG, 6)), dma((PG, 4)), dma((PG, 4)), dma((PG, 4)), dma((PG, 4)),
         ],
@@ -452,15 +452,10 @@
         attend_kernel,
         name="attend",
         out_shape=jax.ShapeDtypeStruct((LR, KVH * QPK * HD), bf),
-        grid=(KVH,),
-        in_specs=[
-            smem, smem, smem,
-            pl.BlockSpec((LR, KVH * QPK * HD), lambda h: (0, 0)),
-            pl.BlockSpec((2, 1, LP + LR, HD), lambda h: (0, h, 0, 0)),
-        ],
-        out_specs=pl.BlockSpec((LR, KVH * QPK * HD), lambda h: (0, 0)),
+        in_specs=[smem, smem, smem, vmem, vmem],
+        out_specs=vmem,
         compiler_params=pltpu.CompilerParams(vmem_limit_bytes=32 << 20),
-    )(prompt_len, owner, resp_len, resp_query, kv)
+    )(prompt_len, owner, resp_len, resp_query, kv.reshape(2, KVH, LP + LR, HD))
 
 
 def solution(mesh):

time: 80 us -> 76.2 us (0.953)
  Pallas kernels: 77.1 us -> 73.3 us
    pallas_call x1, Pallas kernels: 72.6 us -> 69.6 us  [body(): pl.pallas_call(gather_kernel, name='project_and_share', out_shape=jax.Sha...]
    pallas_call x1, Pallas kernels: 4.56 us -> 3.75 us  [body(): pl.pallas_call(attend_kernel, name='attend', out_shape=jax.ShapeDtypeStru...]
where the time goes in v3:
time: 76.2 us; the launch traced here: 76 us
  Pallas kernels  73.3 us (96%)
  between operations  1.35 us (2%)
  local copies, waits for them, and re-layouts  1.32 us (2%)
    pallas_call x1, Pallas kernels, body(): pl.pallas_call(gather_kernel, name='project_and_share', out_shape=jax.Sha...  69.6 us
    pallas_call x1, Pallas kernels, body(): pl.pallas_call(attend_kernel, name='attend', out_shape=jax.ShapeDtypeStru...  3.75 us

profile of v3, /device:TPU:1, one launch (start us, length us, event | category | flops | bytes accessed | tf_op | source)
XLA Modules:
  0.0 76.0 jit_solution(862436658413005428)
XLA Ops:
  1.3 0.0 copy-start.1
  1.3 0.0 copy-start.2
  1.3 69.6 %project_and_share.1 = bf16[2,4,20,2,16,128]{5,4,3,2,1,0:T(8,128)(2,1)} custom-call(bf16[4,16,4096]{2,1,0:T(8,128)(2,1)} %bitcast.7, bf16[8,16,4096]{2,1,0:T(8,128)(2,1)} %bitcast.6, bf16[8,1024]{1,0:T(8,128)(2,1)} %w_ref.1, f32[1,4096]{1,0:T(1,128)} %bitcast.8, f32[1,128]{1,0:T(1,128)} %bitcast.9, f32[1,128]{1,0:T(1,128)} %constant.2.clone.freq_hbm, ...), custom_call_target="tpu_custom_call" | custom-call | tf_op jit(solution)/shard_map/project_and_share/pallas_call | solution.py:416
  70.9 0.0 copy-done.1
  70.9 0.0 copy-done.2
  70.9 0.0 copy-start
  70.9 1.3 %copy-done = bf16[2,4,20,2,16,128]{5,4,3,2,1,0:T(8,128)(2,1)S(1)} copy-done((bf16[2,4,20,2,16,128]{5,4,3,2,1,0:T(8,128)(2,1)S(1)}, bf16[2,4,20,2,16,128]{5,4,3,2,1,0:T(8,128)(2,1)}, u32[]{:S(2)}) %copy-start) | copy-done | bytes 1310744
  72.2 3.7 %attend.1 = bf16[128,2048]{1,0:T(8,128)(2,1)} custom-call(s32[4]{0:T(128)S(1)} %copy-done.2, s32[1]{0:T(128)S(6)} %copy.12.owner_hbm.owner_ref, s32[1]{0:T(128)S(6)} %copy.11.rlen_ref, bf16[128,2048]{1,0:T(8,128)(2,1)S(1)} %copy-done.1, bf16[2,4,640,128]{3,2,1,0:T(8,128)(2,1)S(1)} %bitcast.5), custom_call_target="tpu_custom_call" | custom-call | tf_op jit(solution)/shard_map/attend/pallas_call | solution.py:451
Async XLA Ops:
  1.3 69.6 %copy-start.1 = (bf16[128,2048]{1,0:T(8,128)(2,1)S(1)}, bf16[128,2048]{1,0:T(8,128)(2,1)}, u32[]{:S(2)}) copy-start(bf16[128,2048]{1,0:T(8,128)(2,1)} %q_ref.1) | copy-start | bytes 1572868
  1.3 69.6 %copy-start.2 = (s32[4]{0:T(128)S(1)}, s32[4]{0:T(128)}, u32[]{:S(2)}) copy-start(s32[4]{0:T(128)} %len_ref.1) | copy-start | bytes 52
  70.9 1.3 %copy-start = (bf16[2,4,20,2,16,128]{5,4,3,2,1,0:T(8,128)(2,1)S(1)}, bf16[2,4,20,2,16,128]{5,4,3,2,1,0:T(8,128)(2,1)}, u32[]{:S(2)}) copy-start(bf16[2,4,20,2,16,128]{5,4,3,2,1,0:T(8,128)(2,1)} %project_and_share.1) | copy-start | bytes 3932164

commit v4 on v3

--- a/solution.py
+++ b/solution.py
@@ -126,8 +126,7 @@
     mine, theirs = meta[0:1, :], meta_rx[0:1, :]
     lens = (jnp.where(c == 0, mine, theirs), jnp.where(c == 0, theirs, mine))
 
-    @pl.loop(0, 9)
-    def _(i):
+    def angles(i):
         j = i - 1
         base = jnp.where(i == 0, (32 * (x * NY + y)).astype(jnp.float32), jnp.where(j < 4, lens[0], lens[1]))
         off = jnp.where(i == 0, 0, (j % 4) * 32)
@@ -213,14 +212,20 @@
                 def _():
                     down_copy(t + HOP).start()
 
+            for cp in w2_copies(t)[0::2]:
+                cp.start()
             up_copy(t + 1).wait_recv()
 
             @pl.when(t < 8 - HOP)
             def _():
                 up_copy(t + 1 + HOP).start()
 
-            for cp in w2_copies(t):
+            for cp in w2_copies(t)[1::2]:
                 cp.start()
+
+        @pl.when(jnp.logical_and(t >= 6, t < 15))
+        def _():
+            angles(t - 6)
 
         @pl.when(t < 6)
         def _():

time: 76.2 us -> 76.2 us (level)
  no operation moved by 1% of the time
where the time goes in v4:
time: 76.2 us; the launch traced here: 76 us
  Pallas kernels  73.3 us (96%)
  between operations  1.35 us (2%)
  local copies, waits for them, and re-layouts  1.32 us (2%)
    pallas_call x1, Pallas kernels, body(): pl.pallas_call(gather_kernel, name='project_and_share', out_shape=jax.Sha...  69.6 us
    pallas_call x1, Pallas kernels, body(): pl.pallas_call(attend_kernel, name='attend', out_shape=jax.ShapeDtypeStru...  3.75 us

profile of v4, /device:TPU:1, one launch (start us, length us, event | category | flops | bytes accessed | tf_op | source)
XLA Modules:
  0.0 76.0 jit_solution(9180792708468831892)
XLA Ops:
  1.3 0.0 copy-start.1
  1.3 0.0 copy-start.2
  1.3 69.6 %project_and_share.1 = bf16[2,4,20,2,16,128]{5,4,3,2,1,0:T(8,128)(2,1)} custom-call(bf16[4,16,4096]{2,1,0:T(8,128)(2,1)} %bitcast.7, bf16[8,16,4096]{2,1,0:T(8,128)(2,1)} %bitcast.6, bf16[8,1024]{1,0:T(8,128)(2,1)} %w_ref.1, f32[1,4096]{1,0:T(1,128)} %bitcast.8, f32[1,128]{1,0:T(1,128)} %bitcast.9, f32[1,128]{1,0:T(1,128)} %constant.2.clone.freq_hbm, ...), custom_call_target="tpu_custom_call" | custom-call | tf_op jit(solution)/shard_map/project_and_share/pallas_call | solution.py:421
  70.9 0.0 copy-done.1
  70.9 0.0 copy-done.2
  70.9 0.0 copy-start
  70.9 1.3 %copy-done = bf16[2,4,20,2,16,128]{5,4,3,2,1,0:T(8,128)(2,1)S(1)} copy-done((bf16[2,4,20,2,16,128]{5,4,3,2,1,0:T(8,128)(2,1)S(1)}, bf16[2,4,20,2,16,128]{5,4,3,2,1,0:T(8,128)(2,1)}, u32[]{:S(2)}) %copy-start) | copy-done | bytes 1310744
  72.2 3.7 %attend.1 = bf16[128,2048]{1,0:T(8,128)(2,1)} custom-call(s32[4]{0:T(128)S(1)} %copy-done.2, s32[1]{0:T(128)S(6)} %copy.12.owner_hbm.owner_ref, s32[1]{0:T(128)S(6)} %copy.11.rlen_ref, bf16[128,2048]{1,0:T(8,128)(2,1)S(1)} %copy-done.1, bf16[2,4,640,128]{3,2,1,0:T(8,128)(2,1)S(1)} %bitcast.5), custom_call_target="tpu_custom_call" | custom-call | tf_op jit(solution)/shard_map/attend/pallas_call | solution.py:456
Async XLA Ops:
  1.3 69.6 %copy-start.1 = (bf16[128,2048]{1,0:T(8,128)(2,1)S(1)}, bf16[128,2048]{1,0:T(8,128)(2,1)}, u32[]{:S(2)}) copy-start(bf16[128,2048]{1,0:T(8,128)(2,1)} %q_ref.1) | copy-start | bytes 1572868
  1.3 69.6 %copy-start.2 = (s32[4]{0:T(128)S(1)}, s32[4]{0:T(128)}, u32[]{:S(2)}) copy-start(s32[4]{0:T(128)} %len_ref.1) | copy-start | bytes 52
  70.9 1.3 %copy-start = (bf16[2,4,20,2,16,128]{5,4,3,2,1,0:T(8,128)(2,1)S(1)}, bf16[2,4,20,2,16,128]{5,4,3,2,1,0:T(8,128)(2,1)}, u32[]{:S(2)}) copy-start(bf16[2,4,20,2,16,128]{5,4,3,2,1,0:T(8,128)(2,1)} %project_and_share.1) | copy-start | bytes 3932164
